TPU v7x, 256 devices: a whole 4x4x8 slice. The times are simulated.
256 devices in a mesh: tour: 64 (over x_hi, y, z), rows: 4 (over x_lo, core).
Axes of the slice: x: 4 (x_hi: 2, x_lo: 2; x = x_hi * 2 + x_lo), y: 4, z: 8, core: 2. Of those that a mesh axis runs over, the one named last changes fastest.
Arguments:
- iterate: float32 [16384, 8192], P('rows', 'tour'), may hold values from -32 to 32
- right_vectors: float32 [8192, 8192], P('rows', 'tour'), may hold values from -6 to 6
Outputs:
- rotated_matrix: float32 [16384, 8192], P('rows', 'tour')
- rotated_vectors: float32 [8192, 8192], P('rows', 'tour')
All inputs are finite; a program needn't handle non-finite values.
Results may differ from a plain program's by a relative error of at most 0.0003.
Values sent between devices are 32-bit elements; how exact they have to be, the bound alone decides.
A program may use at most 64 MiB of HBM per device.

v0:
```python
import jax
import jax.numpy as jnp
from jax import lax
from jax.sharding import PartitionSpec as P

ROUNDS = 6


EPSILON = 0.25
HIGHEST = lax.Precision.HIGHEST


def passed_along(shard, axis, by):
    count = lax.axis_size(axis)
    pairs = [(i, i + by) for i in range(count) if 0 <= i + by < count]
    return lax.ppermute(shard, axis, pairs)


def cayley(gram_matrix):
    diag_vals = jnp.diagonal(gram_matrix)
    spread = diag_vals[None, :] - diag_vals[:, None]
    totals = diag_vals[None, :] + diag_vals[:, None]
    skewed = gram_matrix * spread / (spread * spread + EPSILON * totals * totals)
    identity = jnp.eye(gram_matrix.shape[0], dtype=gram_matrix.dtype)
    forward = identity + 0.5 * skewed
    system = identity - 0.25 * jnp.dot(skewed, skewed, precision=HIGHEST)
    factor = jnp.linalg.cholesky(system)
    solved = jax.scipy.linalg.cho_solve((factor, True), forward)
    return jnp.dot(forward, solved, precision=HIGHEST)


def local_gram(left_part, right_part):
    return jnp.einsum("mi,mj->ij", left_part, right_part, precision=HIGHEST)


def outgoing(stacked, half_width, position):
    return jnp.where(position == 0, stacked[:, half_width:], stacked[:, :half_width])


def settle(stacked, half_width, from_left, from_right, position, members):
    upper_half = stacked[:, :half_width]
    new_upper = jnp.where(position == 0, upper_half, from_left)
    new_lower = jnp.where(position == members - 1, upper_half, from_right)
    return jnp.concatenate([new_upper, new_lower], axis=1)


def local(iterate, right_vectors):
    half_width = iterate.shape[1] // 2
    position = lax.axis_index("tour")
    members = lax.axis_size("tour")
    matrix_part = iterate
    vector_part = right_vectors
    for round_index in range(ROUNDS):
        full_gram = lax.psum(local_gram(matrix_part, matrix_part), "rows")
        rotation = cayley(full_gram)
        matrix_part = jnp.dot(matrix_part, rotation, precision=HIGHEST)
        vector_part = jnp.dot(vector_part, rotation, precision=HIGHEST)
        from_left = passed_along(
            (
                outgoing(matrix_part, half_width, position),
                outgoing(vector_part, half_width, position),
            ),
            "tour",
            1,
        )
        from_right = passed_along(
            (matrix_part[:, half_width:], vector_part[:, half_width:]), "tour", -1
        )
        matrix_part = settle(
            matrix_part, half_width, from_left[0], from_right[0], position, members
        )
        vector_part = settle(
            vector_part, half_width, from_left[1], from_right[1], position, members
        )
    return (matrix_part, vector_part)


def solution(mesh):
    placed = (P("rows", "tour"), P("rows", "tour"))
    return jax.shard_map(
        local,
        mesh=mesh,
        in_specs=placed,
        out_specs=(P("rows", "tour"), P("rows", "tour")),
        check_vma=False,
    )
```

profile of v0, /device:TPU:4, one launch (start us, length us, event | category | flops | bytes accessed | tf_op | source)
XLA Modules:
  0.0 712.3 jit_solution(10729624224164267576)
XLA Ops:
  13.1 42.9 %all-reduce.7.cloned.1.call-done = f32[128,128]{0,1:T(8,128)} async-done(((f32[128,128]{0,1:T(8,128)}), f32[128,128]{0,1:T(8,128)}) %all-reduce.7.cloned.1.call-update) | async-done | bytes 65552 | tf_op jit(solution)/shard_map/psum | solution.py:54
  59.3 11.7 %cholesky.104 = f32[128,128]{1,0:T(8,128)S(1)} custom-call(f32[128,128]{1,0:T(8,128)S(1)} %fusion.83), custom_call_target="Cholesky" | custom-call | tf_op jit(solution)/shard_map/jit(cholesky)/cholesky | solution.py:27
  72.4 9.8 %custom-call.24 = f32[1,128,128]{1,2,0:T(8,128)S(1)} custom-call(f32[1,128,128]{2,1,0:T(8,128)S(1)} %fusion.36), custom_call_target="InvertDiagBlocksLowerTriangular" | custom-call | tf_op jit(solution)/shard_map/jit(_cho_solve)/triangular_solve | solution.py:28
  92.0 8.5 %collective-permute-start.1 = (f32[4096,64]{0,1:T(8,128)S(1)}, f32[4096,64]{0,1:T(8,128)}, u32[]{:S(2)}, u32[]{:S(2)}) collective-permute-start(f32[4096,64]{0,1:T(8,128)S(1)} %get-tuple-element.31), channel_id=1, source_target_pairs={{4,0},{8,4},{12,8},{16,12},{20,16},{24,20},{28,24},{32,28},{36,32}... | collective-permute-start | bytes 3145736 | tf_op jit(solution)/shard_map/ppermute | solution.py:16
  103.9 18.0 %collective-permute-done = f32[4096,64]{0,1:T(8,128)} collective-permute-done((f32[4096,64]{0,1:T(8,128)}, f32[4096,64]{0,1:T(8,128)}, u32[]{:S(2)}, u32[]{:S(2)}) %collective-permute-start) | collective-permute-done | bytes 1048608 | tf_op jit(solution)/shard_map/ppermute | solution.py:16
  130.9 10.2 %collective-permute-start.13 = (f32[2048,64]{0,1:T(8,128)}, f32[2048,64]{0,1:T(8,128)}, u32[]{:S(2)}, u32[]{:S(2)}) collective-permute-start(f32[2048,64]{0,1:T(8,128)} %get-tuple-element.55), channel_id=1, source_target_pairs={{4,0},{8,4},{12,8},{16,12},{20,16},{24,20},{28,24},{32,28},{36,32}... | collective-permute-start | bytes 1572872 | tf_op jit(solution)/shard_map/ppermute | solution.py:16
  141.2 31.2 %all-reduce.9.cloned.1.call-done = f32[128,128]{0,1:T(8,128)} async-done(((f32[128,128]{0,1:T(8,128)}), f32[128,128]{0,1:T(8,128)}) %all-reduce.9.cloned.1.call-update) | async-done | bytes 65552 | tf_op jit(solution)/shard_map/psum | solution.py:54
  175.6 11.7 %cholesky.115 = f32[128,128]{1,0:T(8,128)S(1)} custom-call(f32[128,128]{1,0:T(8,128)S(1)} %fusion.78), custom_call_target="Cholesky" | custom-call | tf_op jit(solution)/shard_map/jit(cholesky)/cholesky | solution.py:27
  188.7 9.8 %custom-call.25 = f32[1,128,128]{1,2,0:T(8,128)S(1)} custom-call(f32[1,128,128]{2,1,0:T(8,128)S(1)} %fusion.37), custom_call_target="InvertDiagBlocksLowerTriangular" | custom-call | tf_op jit(solution)/shard_map/jit(_cho_solve)/triangular_solve | solution.py:28
  206.7 8.3 %collective-permute-start.3 = (f32[4096,64]{0,1:T(8,128)S(1)}, f32[4096,64]{0,1:T(8,128)S(1)}, u32[]{:S(2)}, u32[]{:S(2)}) collective-permute-start(f32[4096,64]{0,1:T(8,128)S(1)} %get-tuple-element.27), channel_id=1, source_target_pairs={{4,0},{8,4},{12,8},{16,12},{20,16},{24,20},{28,24},{32,28},{36,32}... | collective-permute-start | bytes 3145736 | tf_op jit(solution)/shard_map/ppermute | solution.py:16
  217.4 18.8 %collective-permute-done.2 = f32[4096,64]{0,1:T(8,128)S(1)} collective-permute-done((f32[4096,64]{0,1:T(8,128)S(1)}, f32[4096,64]{0,1:T(8,128)S(1)}, u32[]{:S(2)}, u32[]{:S(2)}) %collective-permute-start.2) | collective-permute-done | bytes 1048608 | tf_op jit(solution)/shard_map/ppermute | solution.py:16
  243.1 10.1 %collective-permute-start.15 = (f32[2048,64]{0,1:T(8,128)}, f32[2048,64]{0,1:T(8,128)}, u32[]{:S(2)}, u32[]{:S(2)}) collective-permute-start(f32[2048,64]{0,1:T(8,128)} %get-tuple-element.51), channel_id=1, source_target_pairs={{4,0},{8,4},{12,8},{16,12},{20,16},{24,20},{28,24},{32,28},{36,32}... | collective-permute-start | bytes 1572872 | tf_op jit(solution)/shard_map/ppermute | solution.py:16
  253.2 31.2 %all-reduce.11.cloned.1.call-done = f32[128,128]{0,1:T(8,128)} async-done(((f32[128,128]{0,1:T(8,128)}), f32[128,128]{0,1:T(8,128)}) %all-reduce.11.cloned.1.call-update) | async-done | bytes 65552 | tf_op jit(solution)/shard_map/psum | solution.py:54
  287.7 11.7 %cholesky.126 = f32[128,128]{1,0:T(8,128)S(1)} custom-call(f32[128,128]{1,0:T(8,128)S(1)} %fusion.73), custom_call_target="Cholesky" | custom-call | tf_op jit(solution)/shard_map/jit(cholesky)/cholesky | solution.py:27
  300.7 9.8 %custom-call.26 = f32[1,128,128]{1,2,0:T(8,128)S(1)} custom-call(f32[1,128,128]{2,1,0:T(8,128)S(1)} %fusion.38), custom_call_target="InvertDiagBlocksLowerTriangular" | custom-call | tf_op jit(solution)/shard_map/jit(_cho_solve)/triangular_solve | solution.py:28
  318.8 8.5 %collective-permute-start.5 = (f32[4096,64]{0,1:T(8,128)S(1)}, f32[4096,64]{0,1:T(8,128)S(1)}, u32[]{:S(2)}, u32[]{:S(2)}) collective-permute-start(f32[4096,64]{0,1:T(8,128)S(1)} %get-tuple-element.23), channel_id=1, source_target_pairs={{4,0},{8,4},{12,8},{16,12},{20,16},{24,20},{28,24},{32,28},{36,32}... | collective-permute-start | bytes 3145736 | tf_op jit(solution)/shard_map/ppermute | solution.py:16
  329.7 18.6 %collective-permute-done.4 = f32[4096,64]{0,1:T(8,128)S(1)} collective-permute-done((f32[4096,64]{0,1:T(8,128)S(1)}, f32[4096,64]{0,1:T(8,128)S(1)}, u32[]{:S(2)}, u32[]{:S(2)}) %collective-permute-start.4) | collective-permute-done | bytes 1048608 | tf_op jit(solution)/shard_map/ppermute | solution.py:16
  355.1 10.1 %collective-permute-start.17 = (f32[2048,64]{0,1:T(8,128)}, f32[2048,64]{0,1:T(8,128)}, u32[]{:S(2)}, u32[]{:S(2)}) collective-permute-start(f32[2048,64]{0,1:T(8,128)} %get-tuple-element.47), channel_id=1, source_target_pairs={{4,0},{8,4},{12,8},{16,12},{20,16},{24,20},{28,24},{32,28},{36,32}... | collective-permute-start | bytes 1572872 | tf_op jit(solution)/shard_map/ppermute | solution.py:16
  365.2 31.1 %all-reduce.13.cloned.1.call-done = f32[128,128]{0,1:T(8,128)} async-done(((f32[128,128]{0,1:T(8,128)}), f32[128,128]{0,1:T(8,128)}) %all-reduce.13.cloned.1.call-update) | async-done | bytes 65552 | tf_op jit(solution)/shard_map/psum | solution.py:54
  399.7 11.7 %cholesky.137 = f32[128,128]{1,0:T(8,128)S(1)} custom-call(f32[128,128]{1,0:T(8,128)S(1)} %fusion.68), custom_call_target="Cholesky" | custom-call | tf_op jit(solution)/shard_map/jit(cholesky)/cholesky | solution.py:27
  412.7 9.8 %custom-call.27 = f32[1,128,128]{1,2,0:T(8,128)S(1)} custom-call(f32[1,128,128]{2,1,0:T(8,128)S(1)} %fusion.39), custom_call_target="InvertDiagBlocksLowerTriangular" | custom-call | tf_op jit(solution)/shard_map/jit(_cho_solve)/triangular_solve | solution.py:28
  441.5 18.8 %collective-permute-done.6 = f32[4096,64]{0,1:T(8,128)S(1)} collective-permute-done((f32[4096,64]{0,1:T(8,128)S(1)}, f32[4096,64]{0,1:T(8,128)S(1)}, u32[]{:S(2)}, u32[]{:S(2)}) %collective-permute-start.6) | collective-permute-done | bytes 1048608 | tf_op jit(solution)/shard_map/ppermute | solution.py:16
  467.1 10.1 %collective-permute-start.19 = (f32[2048,64]{0,1:T(8,128)}, f32[2048,64]{0,1:T(8,128)}, u32[]{:S(2)}, u32[]{:S(2)}) collective-permute-start(f32[2048,64]{0,1:T(8,128)} %get-tuple-element.43), channel_id=1, source_target_pairs={{4,0},{8,4},{12,8},{16,12},{20,16},{24,20},{28,24},{32,28},{36,32}... | collective-permute-start | bytes 1572872 | tf_op jit(solution)/shard_map/ppermute | solution.py:16
  477.3 31.2 %all-reduce.15.cloned.1.call-done = f32[128,128]{0,1:T(8,128)} async-done(((f32[128,128]{0,1:T(8,128)}), f32[128,128]{0,1:T(8,128)}) %all-reduce.15.cloned.1.call-update) | async-done | bytes 65552 | tf_op jit(solution)/shard_map/psum | solution.py:54
  511.7 11.7 %cholesky.148 = f32[128,128]{1,0:T(8,128)S(1)} custom-call(f32[128,128]{1,0:T(8,128)S(1)} %fusion.63), custom_call_target="Cholesky" | custom-call | tf_op jit(solution)/shard_map/jit(cholesky)/cholesky | solution.py:27
  524.7 9.8 %custom-call.28 = f32[1,128,128]{1,2,0:T(8,128)S(1)} custom-call(f32[1,128,128]{2,1,0:T(8,128)S(1)} %fusion.40), custom_call_target="InvertDiagBlocksLowerTriangular" | custom-call | tf_op jit(solution)/shard_map/jit(_cho_solve)/triangular_solve | solution.py:28
  556.1 9.9 %collective-permute-start.21 = (f32[2048,64]{0,1:T(8,128)S(1)}, f32[2048,64]{0,1:T(8,128)}, u32[]{:S(2)}, u32[]{:S(2)}) collective-permute-start(f32[2048,64]{0,1:T(8,128)S(1)} %get-tuple-element.39), channel_id=1, source_target_pairs={{4,0},{8,4},{12,8},{16,12},{20,16},{24,20},{28,24},{32,28},{36,32}... | collective-permute-start | bytes 1572872 | tf_op jit(solution)/shard_map/ppermute | solution.py:16
  586.9 32.0 %all-reduce.17.cloned.1.call-done = f32[128,128]{0,1:T(8,128)} async-done(((f32[128,128]{0,1:T(8,128)}), f32[128,128]{0,1:T(8,128)}) %all-reduce.17.cloned.1.call-update) | async-done | bytes 65552 | tf_op jit(solution)/shard_map/psum | solution.py:54
  622.2 11.7 %cholesky.159 = f32[128,128]{1,0:T(8,128)S(1)} custom-call(f32[128,128]{1,0:T(8,128)S(1)} %fusion.58), custom_call_target="Cholesky" | custom-call | tf_op jit(solution)/shard_map/jit(cholesky)/cholesky | solution.py:27
  635.1 9.8 %custom-call.29 = f32[1,128,128]{1,2,0:T(8,128)S(1)} custom-call(f32[1,128,128]{2,1,0:T(8,128)S(1)} %fusion.41), custom_call_target="InvertDiagBlocksLowerTriangular" | custom-call | tf_op jit(solution)/shard_map/jit(_cho_solve)/triangular_solve | solution.py:28
  667.1 9.6 %collective-permute-start.11 = (f32[4096,64]{0,1:T(8,128)}, f32[4096,64]{0,1:T(8,128)}, u32[]{:S(2)}, u32[]{:S(2)}) collective-permute-start(f32[4096,64]{0,1:T(8,128)} %get-tuple-element.11), channel_id=1, source_target_pairs={{4,0},{8,4},{12,8},{16,12},{20,16},{24,20},{28,24},{32,28},{36,32}... | collective-permute-start | bytes 3145736 | tf_op jit(solution)/shard_map/ppermute | solution.py:16
  678.3 19.6 %collective-permute-done.10 = f32[4096,64]{0,1:T(8,128)} collective-permute-done((f32[4096,64]{0,1:T(8,128)}, f32[4096,64]{0,1:T(8,128)}, u32[]{:S(2)}, u32[]{:S(2)}) %collective-permute-start.10) | collective-permute-done | bytes 1048608 | tf_op jit(solution)/shard_map/ppermute | solution.py:16
  (171 shorter events, 189.0 us)
Async XLA Ops:
  7.2 48.9 %all-reduce.7.cloned.1.call-start = ((), (), s32[]{:S(2)}) async-start(), calls=%async_computation | async-start | bytes 131072 | tf_op jit(solution)/shard_map/psum | solution.py:54
  12.9 159.5 %all-reduce.9.cloned.1.call-start = ((), (), s32[]{:S(2)}) async-start(), calls=%async_computation.1 | async-start | bytes 131072 | tf_op jit(solution)/shard_map/psum | solution.py:54
  88.4 34.3 %copy-start.3 = (f32[4096,128]{0,1:T(8,128)S(1)}, f32[4096,128]{0,1:T(8,128)}, u32[]{:S(2)}) copy-start(f32[4096,128]{0,1:T(8,128)} %copy-done.2) | copy-start | bytes 6291460
  88.5 33.4 %collective-permute-start = (f32[4096,64]{0,1:T(8,128)}, f32[4096,64]{0,1:T(8,128)}, u32[]{:S(2)}, u32[]{:S(2)}) collective-permute-start(f32[4096,64]{0,1:T(8,128)} %get-tuple-element.30), channel_id=1, source_target_pairs={{0,4},{4,8},{8,12},{12,16},{16,20},{20,24},{24,28},{28,32},{32,36}... | collective-permute-start | bytes 3145736 | tf_op jit(solution)/shard_map/ppermute | solution.py:16
  92.0 30.7 %collective-permute-start.1 = (f32[4096,64]{0,1:T(8,128)S(1)}, f32[4096,64]{0,1:T(8,128)}, u32[]{:S(2)}, u32[]{:S(2)}) collective-permute-start(f32[4096,64]{0,1:T(8,128)S(1)} %get-tuple-element.31), channel_id=1, source_target_pairs={{4,0},{8,4},{12,8},{16,12},{20,16},{24,20},{28,24},{32,28},{36,32}... | collective-permute-start | bytes 3145736 | tf_op jit(solution)/shard_map/ppermute | solution.py:16
  127.9 73.2 %copy-start.5 = (f32[4096,64]{0,1:T(8,128)S(1)}, f32[4096,64]{0,1:T(8,128)}, u32[]{:S(2)}) copy-start(f32[4096,64]{0,1:T(8,128)} %copy-done.4) | copy-start | bytes 3145732
  127.9 156.5 %all-reduce.11.cloned.1.call-start = ((), (), s32[]{:S(2)}) async-start(), calls=%async_computation.2 | async-start | bytes 131072 | tf_op jit(solution)/shard_map/psum | solution.py:54
  129.0 86.0 %collective-permute-start.12 = (f32[2048,64]{0,1:T(8,128)}, f32[2048,64]{0,1:T(8,128)}, u32[]{:S(2)}, u32[]{:S(2)}) collective-permute-start(f32[2048,64]{0,1:T(8,128)} %get-tuple-element.54), channel_id=1, source_target_pairs={{0,4},{4,8},{8,12},{12,16},{16,20},{20,24},{24,28},{28,32},{32,36}... | collective-permute-start | bytes 1572872 | tf_op jit(solution)/shard_map/ppermute | solution.py:16
  130.9 84.1 %collective-permute-start.13 = (f32[2048,64]{0,1:T(8,128)}, f32[2048,64]{0,1:T(8,128)}, u32[]{:S(2)}, u32[]{:S(2)}) collective-permute-start(f32[2048,64]{0,1:T(8,128)} %get-tuple-element.55), channel_id=1, source_target_pairs={{4,0},{8,4},{12,8},{16,12},{20,16},{24,20},{28,24},{32,28},{36,32}... | collective-permute-start | bytes 1572872 | tf_op jit(solution)/shard_map/ppermute | solution.py:16
  203.3 33.0 %collective-permute-start.2 = (f32[4096,64]{0,1:T(8,128)S(1)}, f32[4096,64]{0,1:T(8,128)S(1)}, u32[]{:S(2)}, u32[]{:S(2)}) collective-permute-start(f32[4096,64]{0,1:T(8,128)S(1)} %get-tuple-element.26), channel_id=1, source_target_pairs={{0,4},{4,8},{8,12},{12,16},{16,20},{20,24},{24,28},{28,32},{32,36}... | collective-permute-start | bytes 3145736 | tf_op jit(solution)/shard_map/ppermute | solution.py:16
  206.7 30.7 %collective-permute-start.3 = (f32[4096,64]{0,1:T(8,128)S(1)}, f32[4096,64]{0,1:T(8,128)S(1)}, u32[]{:S(2)}, u32[]{:S(2)}) collective-permute-start(f32[4096,64]{0,1:T(8,128)S(1)} %get-tuple-element.27), channel_id=1, source_target_pairs={{4,0},{8,4},{12,8},{16,12},{20,16},{24,20},{28,24},{32,28},{36,32}... | collective-permute-start | bytes 3145736 | tf_op jit(solution)/shard_map/ppermute | solution.py:16
  240.1 156.3 %all-reduce.13.cloned.1.call-start = ((), (), s32[]{:S(2)}) async-start(), calls=%async_computation.3 | async-start | bytes 131072 | tf_op jit(solution)/shard_map/psum | solution.py:54
  241.2 86.1 %collective-permute-start.14 = (f32[2048,64]{0,1:T(8,128)}, f32[2048,64]{0,1:T(8,128)}, u32[]{:S(2)}, u32[]{:S(2)}) collective-permute-start(f32[2048,64]{0,1:T(8,128)} %get-tuple-element.50), channel_id=1, source_target_pairs={{0,4},{4,8},{8,12},{12,16},{16,20},{20,24},{24,28},{28,32},{32,36}... | collective-permute-start | bytes 1572872 | tf_op jit(solution)/shard_map/ppermute | solution.py:16
  243.1 84.2 %collective-permute-start.15 = (f32[2048,64]{0,1:T(8,128)}, f32[2048,64]{0,1:T(8,128)}, u32[]{:S(2)}, u32[]{:S(2)}) collective-permute-start(f32[2048,64]{0,1:T(8,128)} %get-tuple-element.51), channel_id=1, source_target_pairs={{4,0},{8,4},{12,8},{16,12},{20,16},{24,20},{28,24},{32,28},{36,32}... | collective-permute-start | bytes 1572872 | tf_op jit(solution)/shard_map/ppermute | solution.py:16
  315.3 33.0 %collective-permute-start.4 = (f32[4096,64]{0,1:T(8,128)S(1)}, f32[4096,64]{0,1:T(8,128)S(1)}, u32[]{:S(2)}, u32[]{:S(2)}) collective-permute-start(f32[4096,64]{0,1:T(8,128)S(1)} %get-tuple-element.22), channel_id=1, source_target_pairs={{0,4},{4,8},{8,12},{12,16},{16,20},{20,24},{24,28},{28,32},{32,36}... | collective-permute-start | bytes 3145736 | tf_op jit(solution)/shard_map/ppermute | solution.py:16
  318.8 30.7 %collective-permute-start.5 = (f32[4096,64]{0,1:T(8,128)S(1)}, f32[4096,64]{0,1:T(8,128)S(1)}, u32[]{:S(2)}, u32[]{:S(2)}) collective-permute-start(f32[4096,64]{0,1:T(8,128)S(1)} %get-tuple-element.23), channel_id=1, source_target_pairs={{4,0},{8,4},{12,8},{16,12},{20,16},{24,20},{28,24},{32,28},{36,32}... | collective-permute-start | bytes 3145736 | tf_op jit(solution)/shard_map/ppermute | solution.py:16
  352.1 156.3 %all-reduce.15.cloned.1.call-start = ((), (), s32[]{:S(2)}) async-start(), calls=%async_computation.4 | async-start | bytes 131072 | tf_op jit(solution)/shard_map/psum | solution.py:54
  353.2 85.8 %collective-permute-start.16 = (f32[2048,64]{0,1:T(8,128)}, f32[2048,64]{0,1:T(8,128)}, u32[]{:S(2)}, u32[]{:S(2)}) collective-permute-start(f32[2048,64]{0,1:T(8,128)} %get-tuple-element.46), channel_id=1, source_target_pairs={{0,4},{4,8},{8,12},{12,16},{16,20},{20,24},{24,28},{28,32},{32,36}... | collective-permute-start | bytes 1572872 | tf_op jit(solution)/shard_map/ppermute | solution.py:16
  355.1 83.9 %collective-permute-start.17 = (f32[2048,64]{0,1:T(8,128)}, f32[2048,64]{0,1:T(8,128)}, u32[]{:S(2)}, u32[]{:S(2)}) collective-permute-start(f32[2048,64]{0,1:T(8,128)} %get-tuple-element.47), channel_id=1, source_target_pairs={{4,0},{8,4},{12,8},{16,12},{20,16},{24,20},{28,24},{32,28},{36,32}... | collective-permute-start | bytes 1572872 | tf_op jit(solution)/shard_map/ppermute | solution.py:16
  427.3 33.0 %collective-permute-start.6 = (f32[4096,64]{0,1:T(8,128)S(1)}, f32[4096,64]{0,1:T(8,128)S(1)}, u32[]{:S(2)}, u32[]{:S(2)}) collective-permute-start(f32[4096,64]{0,1:T(8,128)S(1)} %get-tuple-element.18), channel_id=1, source_target_pairs={{0,4},{4,8},{8,12},{12,16},{16,20},{20,24},{24,28},{28,32},{32,36}... | collective-permute-start | bytes 3145736 | tf_op jit(solution)/shard_map/ppermute | solution.py:16
  430.8 30.7 %collective-permute-start.7 = (f32[4096,64]{0,1:T(8,128)S(1)}, f32[4096,64]{0,1:T(8,128)S(1)}, u32[]{:S(2)}, u32[]{:S(2)}) collective-permute-start(f32[4096,64]{0,1:T(8,128)S(1)} %get-tuple-element.19), channel_id=1, source_target_pairs={{4,0},{8,4},{12,8},{16,12},{20,16},{24,20},{28,24},{32,28},{36,32}... | collective-permute-start | bytes 3145736 | tf_op jit(solution)/shard_map/ppermute | solution.py:16
  464.1 154.8 %all-reduce.17.cloned.1.call-start = ((), (), s32[]{:S(2)}) async-start(), calls=%async_computation.5 | async-start | bytes 131072 | tf_op jit(solution)/shard_map/psum | solution.py:54
  465.2 85.7 %collective-permute-start.18 = (f32[2048,64]{0,1:T(8,128)}, f32[2048,64]{0,1:T(8,128)}, u32[]{:S(2)}, u32[]{:S(2)}) collective-permute-start(f32[2048,64]{0,1:T(8,128)} %get-tuple-element.42), channel_id=1, source_target_pairs={{0,4},{4,8},{8,12},{12,16},{16,20},{20,24},{24,28},{28,32},{32,36}... | collective-permute-start | bytes 1572872 | tf_op jit(solution)/shard_map/ppermute | solution.py:16
  467.1 83.8 %collective-permute-start.19 = (f32[2048,64]{0,1:T(8,128)}, f32[2048,64]{0,1:T(8,128)}, u32[]{:S(2)}, u32[]{:S(2)}) collective-permute-start(f32[2048,64]{0,1:T(8,128)} %get-tuple-element.43), channel_id=1, source_target_pairs={{4,0},{8,4},{12,8},{16,12},{20,16},{24,20},{28,24},{32,28},{36,32}... | collective-permute-start | bytes 1572872 | tf_op jit(solution)/shard_map/ppermute | solution.py:16
  539.3 33.6 %collective-permute-start.8 = (f32[4096,64]{0,1:T(8,128)S(1)}, f32[4096,64]{0,1:T(8,128)S(1)}, u32[]{:S(2)}, u32[]{:S(2)}) collective-permute-start(f32[4096,64]{0,1:T(8,128)S(1)} %get-tuple-element.14), channel_id=1, source_target_pairs={{0,4},{4,8},{8,12},{12,16},{16,20},{20,24},{24,28},{28,32},{32,36}... | collective-permute-start | bytes 3145736 | tf_op jit(solution)/shard_map/ppermute | solution.py:16
  542.8 31.6 %collective-permute-start.9 = (f32[4096,64]{0,1:T(8,128)S(1)}, f32[4096,64]{0,1:T(8,128)S(1)}, u32[]{:S(2)}, u32[]{:S(2)}) collective-permute-start(f32[4096,64]{0,1:T(8,128)S(1)} %get-tuple-element.15), channel_id=1, source_target_pairs={{4,0},{8,4},{12,8},{16,12},{20,16},{24,20},{28,24},{32,28},{36,32}... | collective-permute-start | bytes 3145736 | tf_op jit(solution)/shard_map/ppermute | solution.py:16
  554.2 29.4 %collective-permute-start.20 = (f32[2048,64]{0,1:T(8,128)}, f32[2048,64]{0,1:T(8,128)S(1)}, u32[]{:S(2)}, u32[]{:S(2)}) collective-permute-start(f32[2048,64]{0,1:T(8,128)} %get-tuple-element.38), channel_id=1, source_target_pairs={{0,4},{4,8},{8,12},{12,16},{16,20},{20,24},{24,28},{28,32},{32,36}... | collective-permute-start | bytes 1572872 | tf_op jit(solution)/shard_map/ppermute | solution.py:16
  556.1 28.6 %collective-permute-start.21 = (f32[2048,64]{0,1:T(8,128)S(1)}, f32[2048,64]{0,1:T(8,128)}, u32[]{:S(2)}, u32[]{:S(2)}) collective-permute-start(f32[2048,64]{0,1:T(8,128)S(1)} %get-tuple-element.39), channel_id=1, source_target_pairs={{4,0},{8,4},{12,8},{16,12},{20,16},{24,20},{28,24},{32,28},{36,32}... | collective-permute-start | bytes 1572872 | tf_op jit(solution)/shard_map/ppermute | solution.py:16
  652.1 24.6 %collective-permute-start.22 = (f32[2048,64]{0,1:T(8,128)S(1)}, f32[2048,64]{0,1:T(8,128)S(1)}, u32[]{:S(2)}, u32[]{:S(2)}) collective-permute-start(f32[2048,64]{0,1:T(8,128)S(1)} %get-tuple-element.34), channel_id=1, source_target_pairs={{0,4},{4,8},{8,12},{12,16},{16,20},{20,24},{24,28},{28,32},{32,36}... | collective-permute-start | bytes 1572872 | tf_op jit(solution)/shard_map/ppermute | solution.py:16
  655.6 21.2 %collective-permute-start.23 = (f32[2048,64]{0,1:T(8,128)S(1)}, f32[2048,64]{0,1:T(8,128)S(1)}, u32[]{:S(2)}, u32[]{:S(2)}) collective-permute-start(f32[2048,64]{0,1:T(8,128)S(1)} %get-tuple-element.35), channel_id=1, source_target_pairs={{4,0},{8,4},{12,8},{16,12},{20,16},{24,20},{28,24},{32,28},{36,32}... | collective-permute-start | bytes 1572872 | tf_op jit(solution)/shard_map/ppermute | solution.py:16
  665.2 32.8 %collective-permute-start.10 = (f32[4096,64]{0,1:T(8,128)}, f32[4096,64]{0,1:T(8,128)}, u32[]{:S(2)}, u32[]{:S(2)}) collective-permute-start(f32[4096,64]{0,1:T(8,128)} %get-tuple-element.10), channel_id=1, source_target_pairs={{0,4},{4,8},{8,12},{12,16},{16,20},{20,24},{24,28},{28,32},{32,36}... | collective-permute-start | bytes 3145736 | tf_op jit(solution)/shard_map/ppermute | solution.py:16
  667.1 32.0 %collective-permute-start.11 = (f32[4096,64]{0,1:T(8,128)}, f32[4096,64]{0,1:T(8,128)}, u32[]{:S(2)}, u32[]{:S(2)}) collective-permute-start(f32[4096,64]{0,1:T(8,128)} %get-tuple-element.11), channel_id=1, source_target_pairs={{4,0},{8,4},{12,8},{16,12},{20,16},{24,20},{28,24},{32,28},{36,32}... | collective-permute-start | bytes 3145736 | tf_op jit(solution)/shard_map/ppermute | solution.py:16
  (7 other events, 18.8 us)
Sparse Core Ops, SparseCore 0:
  13.0 42.9 all-reduce.6
  128.0 44.2 all-reduce.8
  240.2 44.1 all-reduce.10
  352.2 44.1 all-reduce.12
  464.2 44.1 all-reduce.14
  579.9 38.9 all-reduce.16
where the time goes:
time: 718 us; the launch traced here: 712 us
  waiting for transfers between devices  313 us (44%)
  other arithmetic  160 us (22%)
  starting transfers between devices  143 us (20%)
  matrix products  62.8 us (9%)
  local copies, waits for them, and re-layouts  19.3 us (3%)
  between operations  15.3 us (2%)
    psum x6, waiting for transfers between devices, local(): full_gram = lax.psum(local_gram(matrix_part, matrix_part), 'rows')  200 us
    ppermute x24, starting transfers between devices, passed_along(): return lax.ppermute(shard, axis, pairs)  142 us
    ppermute x24, waiting for transfers between devices, passed_along(): return lax.ppermute(shard, axis, pairs)  113 us
    another operation x18, other arithmetic, cayley(): factor = jnp.linalg.cholesky(system)  74.4 us
    another operation x12, other arithmetic, cayley(): solved = jax.scipy.linalg.cho_solve((factor, True), forward)  62.6 us
    dot_general x6, matrix products, local_gram(): return jnp.einsum('mi,mj->ij', left_part, right_part, precision=HIGHEST)  17.9 us
  transfers between devices with their start and end apart: 30, of which 20 were waited for; matrix products, arithmetic and copies ran while one was open for 21% of the time, Pallas kernels for 0%

commit v1 on v0

v1 whole, which is shorter than its diff:
```python
import functools

import jax
import jax.numpy as jnp
from jax import lax
from jax.experimental import pallas as pl
from jax.experimental.pallas import tpu as pltpu
from jax.sharding import PartitionSpec as P

ROUNDS = 6
EPSILON = 0.25
CHUNK = 512
HALF = 64
WIDE = 128
TOP_EIGENVALUE = 336.0
NEWTON_STEPS = 7
MESH = pl.DeviceIdType.MESH


def split(value):
    high = value.astype(jnp.bfloat16)
    return high, (value - high.astype(jnp.float32)).astype(jnp.bfloat16)


def product(left, right):
    dot = functools.partial(jnp.dot, preferred_element_type=jnp.float32)
    return dot(left[0], right[0]) + (dot(left[0], right[1]) + dot(left[1], right[0]))


def exact(left, right):
    return jnp.dot(
        left, right, precision=lax.Precision.HIGHEST, preferred_element_type=jnp.float32)


def rotation_of(gram):
    down = lax.broadcasted_iota(jnp.int32, (WIDE, WIDE), 0)
    across = lax.broadcasted_iota(jnp.int32, (WIDE, WIDE), 1)
    on_diagonal = down == across
    diagonal = jnp.where(on_diagonal, gram, 0.0)
    along = jnp.sum(diagonal, axis=0, keepdims=True)
    upright = jnp.sum(diagonal, axis=1, keepdims=True)
    spread = along - upright
    totals = along + upright
    half = 0.5 * (gram * spread / (spread * spread + EPSILON * totals * totals))
    identity = jnp.where(on_diagonal, 1.0, 0.0).astype(jnp.float32)
    system = identity - exact(half, half)
    scale = 2.0 / (1.0 + TOP_EIGENVALUE)
    error = (TOP_EIGENVALUE - 1.0) / (TOP_EIGENVALUE + 1.0)
    image = scale * system
    inverse = None
    for step in range(NEWTON_STEPS):
        gain = 2.0 / (2.0 - error * error)
        error = error * error / (2.0 - error * error)
        factor = gain * (2.0 * identity - image)
        factor_split = split(factor)
        if inverse is None:
            inverse = scale * factor
        else:
            inverse = product(split(inverse), factor_split)
        if step < NEWTON_STEPS - 1:
            image = product(split(image), factor_split)
    residual = 2.0 * identity - exact(system, inverse)
    forward = exact(identity + half, inverse)
    return 2.0 * exact(forward, residual) - identity


def kernel(
    matrix_in, vectors_in, matrix_out, vectors_out,
    upper, lower, stage, sums, spun, grams,
    load_sem, store_sem, sent_sem, come_sem, gram_sent, gram_come,
):
    slot = lax.axis_index("tour")
    members = lax.axis_size("tour")
    share = lax.axis_index("rows")
    first = slot == 0
    last = slot == members - 1
    crossing = jnp.logical_or(slot == members // 2 - 1, slot == members // 2)
    peers = (share + 1 - 2 * lax.rem(share, 2), lax.rem(share + 2, 4), 3 - share)
    tall = matrix_in.shape[0] // 2
    flat = vectors_in.shape[0] // 2
    chunks = tall // CHUNK
    every = (tall + flat) // CHUNK
    lane = lax.broadcasted_iota(jnp.int32, (CHUNK, WIDE), 1)
    near = lane < HALF

    def rows(c):
        return pl.ds(pl.multiple_of(c * CHUNK, CHUNK), CHUNK)

    def load(part):
        if part == 0:
            return pltpu.make_async_copy(
                matrix_in, stage.at[pl.ds(0, 2 * tall)], load_sem.at[0])
        return pltpu.make_async_copy(
            vectors_in, stage.at[pl.ds(2 * tall, 2 * flat)], load_sem.at[1])

    load(0).start()
    load(1).start()

    barrier = pltpu.get_barrier_semaphore()
    for peer in peers:
        pl.semaphore_signal(barrier, inc=1, device_id={"rows": peer}, device_id_type=MESH)

    @pl.when(jnp.logical_not(first))
    def _():
        pl.semaphore_signal(barrier, inc=1, device_id={"tour": slot - 1}, device_id_type=MESH)

    @pl.when(jnp.logical_not(last))
    def _():
        pl.semaphore_signal(barrier, inc=1, device_id={"tour": slot + 1}, device_id_type=MESH)

    def rightward(r, c):
        return pltpu.make_async_remote_copy(
            upper.at[r, rows(c)], upper.at[r + 1, rows(c)],
            sent_sem.at[0, r, c], come_sem.at[0, r, c],
            device_id={"tour": slot + 1}, device_id_type=MESH)

    def leftward(r, c):
        return pltpu.make_async_remote_copy(
            lower.at[r, rows(c)], lower.at[r + 1, rows(c)],
            sent_sem.at[1, r, c], come_sem.at[1, r, c],
            device_id={"tour": slot - 1}, device_id_type=MESH)

    def turn_first(r, c):
        return pltpu.make_async_copy(
            lower.at[r, rows(c)], upper.at[r + 1, rows(c)], come_sem.at[0, r, c])

    def turn_last(r, c):
        return pltpu.make_async_copy(
            upper.at[r, rows(c)], lower.at[r + 1, rows(c)], come_sem.at[1, r, c])

    def send(r, c):
        @pl.when(last)
        def _():
            turn_last(r, c).start()

        @pl.when(jnp.logical_not(last))
        def _():
            rightward(r, c).start()

        @pl.when(first)
        def _():
            turn_first(r, c).start()

        @pl.when(jnp.logical_not(first))
        def _():
            leftward(r, c).start()

    def receive(r, c):
        @pl.when(first)
        def _():
            turn_first(r, c).wait()

        @pl.when(jnp.logical_not(first))
        def _():
            rightward(r, c).wait_recv()

        @pl.when(last)
        def _():
            turn_last(r, c).wait()

        @pl.when(jnp.logical_not(last))
        def _():
            leftward(r, c).wait_recv()

    def staged(c):
        start = jnp.where(c < chunks, c * CHUNK, 2 * tall + (c - chunks) * CHUNK)
        skip = jnp.where(c < chunks, tall, flat)
        return (
            pl.ds(pl.multiple_of(start, CHUNK), CHUNK),
            pl.ds(pl.multiple_of(start + skip, CHUNK), CHUNK),
        )

    def pack(c, _):
        one, two = staged(c)
        one, two = stage[one], stage[two]
        upper[0, rows(c)] = jnp.where(near, one, pltpu.roll(two, HALF, 1))
        lower[0, rows(c)] = jnp.where(near, pltpu.roll(one, HALF, 1), two)
        return 0

    def add_gram(r, c):
        block = jnp.concatenate([upper[r, rows(c)], lower[r, rows(c)]], axis=1)
        high, low = split(block)
        dims = (((0,), (0,)), ((), ()))
        sums[:, : 2 * WIDE] += lax.dot_general(high, high, dims, preferred_element_type=jnp.float32)
        sums[:, 2 * WIDE :] += lax.dot_general(high, low, dims, preferred_element_type=jnp.float32)

    near_square = lax.broadcasted_iota(jnp.int32, (HALF, WIDE), 1) < HALF

    def folded(at):
        left = sums[:, at : at + WIDE]
        right = sums[:, at + WIDE : at + 2 * WIDE]
        parts = []
        for start in (0, WIDE):
            one, two = slice(start, start + HALF), slice(start + HALF, start + WIDE)
            parts.append(jnp.where(
                near_square,
                left[one] + pltpu.roll(left[two], HALF, 1),
                pltpu.roll(right[one], HALF, 1) + right[two]))
        return jnp.concatenate(parts, axis=0)

    def swap_gram(r, k):
        return pltpu.make_async_remote_copy(
            grams.at[r, share], grams.at[r, share], gram_sent.at[r, k], gram_come.at[r, k],
            device_id={"rows": peers[k]}, device_id_type=MESH)

    def spread_out(rotation):
        columns = []
        for half in (rotation[:HALF], rotation[HALF:]):
            rolled = pltpu.roll(half, HALF, 1)
            columns.append((
                jnp.concatenate([jnp.where(near_square, half, 0.0), jnp.where(near_square, 0.0, rolled)], axis=0),
                jnp.concatenate([jnp.where(near_square, rolled, 0.0), jnp.where(near_square, 0.0, half)], axis=0)))
        to_upper = jnp.concatenate([columns[0][0], columns[1][0]], axis=0)
        to_lower = jnp.concatenate([columns[0][1], columns[1][1]], axis=0)
        return jnp.concatenate(
            [jnp.where(first, to_lower, to_upper), jnp.where(first, to_upper, to_lower)], axis=1)

    def turn(r, c):
        block = jnp.concatenate([upper[r, rows(c)], lower[r, rows(c)]], axis=1)
        result = product(split(block), (spun[0], spun[1]))
        upper[r, rows(c)] = result[:, :WIDE]
        lower[r, rows(c)] = result[:, WIDE:]

    def gram_step(r):
        def step(c, _):
            @pl.when(r > 0)
            def _():
                receive(r - 1, c)

            add_gram(r, c)
            return 0
        return step

    def matrix_step(r):
        def step(c, _):
            turn(r, c)
            send(r, c)
            return 0
        return step

    def vector_step(r):
        def step(c, _):
            @pl.when(r > 0)
            def _():
                receive(r - 1, c)

            turn(r, c)
            send(r, c)
            return 0
        return step

    load(0).wait()
    lax.fori_loop(0, chunks, pack, 0)

    def one_round(r, _):
        sums[...] = jnp.zeros_like(sums)
        lax.fori_loop(0, chunks, gram_step(r), 0)
        cross = folded(2 * WIDE)
        grams[r, share] = folded(0) + (cross + cross.T)

        @pl.when(r == 0)
        def _():
            @pl.when(jnp.logical_or(first, last))
            def _():
                pl.semaphore_wait(barrier, 4)

            @pl.when(jnp.logical_not(jnp.logical_or(first, last)))
            def _():
                pl.semaphore_wait(barrier, 5)

        for k in range(3):
            swap_gram(r, k).start()

        @pl.when(r == 0)
        def _():
            load(1).wait()
            lax.fori_loop(chunks, every, pack, 0)

        for k in range(3):
            swap_gram(r, k).wait_recv()

        @pl.when(jnp.logical_and(crossing, r > 0))
        def _():
            lax.fori_loop(chunks, every, vector_step(r - 1), 0)

        gram = (grams[r, 0] + grams[r, 1]) + (grams[r, 2] + grams[r, 3])
        spun[0], spun[1] = split(spread_out(rotation_of(gram)))
        lax.fori_loop(0, chunks, matrix_step(r), 0)

        @pl.when(jnp.logical_not(crossing))
        def _():
            lax.fori_loop(chunks, every, vector_step(r), 0)

        return 0

    lax.fori_loop(0, ROUNDS, one_round, 0)

    @pl.when(crossing)
    def _():
        lax.fori_loop(chunks, every, vector_step(ROUNDS - 1), 0)

    def store(c, half):
        piece = staged(c)[half]
        return piece

    def finish(kind, out, offset):
        def step(c, _):
            receive(ROUNDS - 1, c)
            one, two = staged(c)
            high, low = upper[ROUNDS, rows(c)], lower[ROUNDS, rows(c)]
            stage[one] = jnp.where(near, high, pltpu.roll(low, HALF, 1))
            stage[two] = jnp.where(near, pltpu.roll(high, HALF, 1), low)
            for half, piece in enumerate((one, two)):
                base = (c - kind * chunks) * CHUNK + half * offset
                pltpu.make_async_copy(
                    stage.at[piece], out.at[pl.ds(pl.multiple_of(base, CHUNK), CHUNK)],
                    store_sem.at[half, c]).start()
            return 0
        return step

    lax.fori_loop(0, chunks, finish(0, matrix_out, tall), 0)
    lax.fori_loop(chunks, every, finish(1, vectors_out, flat), 0)

    def settle(kind, out, offset):
        def step(c, _):
            for half, piece in enumerate(staged(c)):
                base = (c - kind * chunks) * CHUNK + half * offset
                pltpu.make_async_copy(
                    stage.at[piece], out.at[pl.ds(pl.multiple_of(base, CHUNK), CHUNK)],
                    store_sem.at[half, c]).wait()
            return 0
        return step

    def drain(r, _):
        for k in range(3):
            swap_gram(r, k).wait_send()

        def step(c, _):
            @pl.when(jnp.logical_not(last))
            def _():
                rightward(r, c).wait_send()

            @pl.when(jnp.logical_not(first))
            def _():
                leftward(r, c).wait_send()

            return 0

        lax.fori_loop(0, every, step, 0)
        return 0

    lax.fori_loop(0, ROUNDS, drain, 0)
    lax.fori_loop(0, chunks, settle(0, matrix_out, tall), 0)
    lax.fori_loop(chunks, every, settle(1, vectors_out, flat), 0)


def local(iterate, right_vectors):
    tall, flat = iterate.shape[0] // 2, right_vectors.shape[0] // 2
    every = (tall + flat) // CHUNK
    anywhere = pl.BlockSpec(memory_space=pl.ANY)
    return pl.pallas_call(
        kernel,
        out_shape=(
            jax.ShapeDtypeStruct(iterate.shape, jnp.float32),
            jax.ShapeDtypeStruct(right_vectors.shape, jnp.float32),
        ),
        in_specs=[anywhere, anywhere],
        out_specs=(anywhere, anywhere),
        scratch_shapes=[
            pltpu.VMEM((ROUNDS + 1, tall + flat, WIDE), jnp.float32),
            pltpu.VMEM((ROUNDS + 1, tall + flat, WIDE), jnp.float32),
            pltpu.VMEM((2 * (tall + flat), WIDE), jnp.float32),
            pltpu.VMEM((2 * WIDE, 4 * WIDE), jnp.float32),
            pltpu.VMEM((2, 2 * WIDE, 2 * WIDE), jnp.bfloat16),
            pltpu.VMEM((ROUNDS, 4, WIDE, WIDE), jnp.float32),
            pltpu.SemaphoreType.DMA((2,)),
            pltpu.SemaphoreType.DMA((2, every)),
            pltpu.SemaphoreType.DMA((2, ROUNDS, every)),
            pltpu.SemaphoreType.DMA((2, ROUNDS, every)),
            pltpu.SemaphoreType.DMA((ROUNDS, 3)),
            pltpu.SemaphoreType.DMA((ROUNDS, 3)),
        ],
        compiler_params=pltpu.CompilerParams(
            collective_id=0, has_side_effects=True, vmem_limit_bytes=48 * 2**20),
        cost_estimate=pl.CostEstimate(
            flops=6 * ROUNDS * 2 * 2048 * 256 * 256, bytes_accessed=12 * 2**20, transcendentals=0),
    )(iterate, right_vectors)


def solution(mesh):
    placed = (P("rows", "tour"), P("rows", "tour"))
    return jax.shard_map(
        local, mesh=mesh, in_specs=placed, out_specs=placed, check_vma=False)
```

time: 718 us -> 283 us (0.39)
  waiting for transfers between devices: 313 us -> 0 us
  Pallas kernels: 0 us -> 275 us
  other arithmetic: 160 us -> 0 us
  starting transfers between devices: 143 us -> 0 us
  matrix products: 62.8 us -> 0 us
  local copies, waits for them, and re-layouts: 19.3 us -> 3.51 us
  between operations: 15.3 us -> 0.65 us
    pallas_call x0 -> x1, Pallas kernels: none -> 275 us  [local(): pl.pallas_call(kernel, out_shape=(jax.ShapeDtypeStruct(iterate.shape, jnp...]
    psum x6 -> x0, waiting for transfers between devices: 200 us -> none  [local(): full_gram = lax.psum(local_gram(matrix_part, matrix_part), 'rows')]
    ppermute x24 -> x0, starting transfers between devices: 142 us -> none  [passed_along(): return lax.ppermute(shard, axis, pairs)]
    another operation x30 -> x0, other arithmetic: 137 us -> none  [the longest x18 74.4 us: cayley(): factor = jnp.linalg.cholesky(system)]
    ppermute x24 -> x0, waiting for transfers between devices: 113 us -> none  [passed_along(): return lax.ppermute(shard, axis, pairs)]
    dot_general x30 -> x0, matrix products: 54.4 us -> none  [the longest x6 17.9 us: local_gram(): return jnp.einsum('mi,mj->ij', left_part, right_part, precision=HIGHEST)]
    select_n x24 -> x0, other arithmetic: 21 us -> none  [the longest x12 12.6 us: settle(): new_upper = jnp.where(position == 0, upper_half, from_left)]
    gather x6 -> x0, local copies, waits for them, and re-layouts: 11.7 us -> none  [cayley(): diag_vals = jnp.diagonal(gram_matrix)]
  transfers between devices with their start and end apart: 30 -> 0, of which waited for: 20 -> 0; matrix products, arithmetic and copies ran while one was open for 21% -> 0% of each run, Pallas kernels for 0% -> 0%
where the time goes in v1:
time: 283 us; the launch traced here: 279 us
  Pallas kernels  275 us (97%)
  local copies, waits for them, and re-layouts  3.51 us (1%)
    pallas_call x1, Pallas kernels, local(): pl.pallas_call(kernel, out_shape=(jax.ShapeDtypeStruct(iterate.shape, jnp...  275 us

profile of v1, /device:TPU:4, one launch (start us, length us, event | category | flops | bytes accessed | tf_op | source)
XLA Modules:
  0.0 278.7 jit_solution(8668985489997138181)
XLA Ops:
  0.6 0.0 copy-start
  0.6 1.2 copy-done
  1.9 274.5 %shard_map.41 = (f32[4096,128]{1,0:T(8,128)S(1)}, f32[2048,128]{1,0:T(8,128)S(1)}) custom-call(f32[4096,128]{1,0:T(8,128)} %matrix_in.1, f32[2048,128]{1,0:T(8,128)S(1)} %copy-done), custom_call_target="tpu_custom_call" | custom-call | flops 9663676416 | bytes 12582912 | tf_op jit(solution)/shard_map/pallas_call | solution.py:361
  276.4 1.3 copy.6
  277.7 1.0 copy.7
Async XLA Ops:
  0.6 1.2 copy-start

commit v2 on v1

--- a/solution.py
+++ b/solution.py
@@ -66,15 +66,21 @@
 
 def kernel(
     matrix_in, vectors_in, matrix_out, vectors_out,
-    upper, lower, stage, sums, spun, grams,
-    load_sem, store_sem, sent_sem, come_sem, gram_sent, gram_come,
+    upper, lower, stage, relay, sums, spun, grams,
+    load_sem, store_sem, sent_sem, come_sem, relay_sent, relay_come, gram_sent, gram_come,
 ):
     slot = lax.axis_index("tour")
     members = lax.axis_size("tour")
     share = lax.axis_index("rows")
     first = slot == 0
     last = slot == members - 1
-    crossing = jnp.logical_or(slot == members // 2 - 1, slot == members // 2)
+    ends = jnp.logical_or(first, last)
+    before, after = members // 2 - 1, members // 2
+    leaves_right = slot == before
+    leaves_left = slot == after
+    crossing = jnp.logical_or(leaves_right, leaves_left)
+    next_door = jnp.logical_not(jnp.logical_or(last, leaves_right))
+    next_back = jnp.logical_not(jnp.logical_or(first, leaves_left))
     peers = (share + 1 - 2 * lax.rem(share, 2), lax.rem(share + 2, 4), 3 - share)
     tall = matrix_in.shape[0] // 2
     flat = vectors_in.shape[0] // 2
@@ -100,13 +106,26 @@
     for peer in peers:
         pl.semaphore_signal(barrier, inc=1, device_id={"rows": peer}, device_id_type=MESH)
 
-    @pl.when(jnp.logical_not(first))
+    def greet(other):
+        pl.semaphore_signal(barrier, inc=1, device_id={"tour": other}, device_id_type=MESH)
+
+    @pl.when(next_back)
     def _():
-        pl.semaphore_signal(barrier, inc=1, device_id={"tour": slot - 1}, device_id_type=MESH)
-
-    @pl.when(jnp.logical_not(last))
+        greet(slot - 1)
+
+    @pl.when(next_door)
     def _():
-        pl.semaphore_signal(barrier, inc=1, device_id={"tour": slot + 1}, device_id_type=MESH)
+        greet(slot + 1)
+
+    @pl.when(ends)
+    def _():
+        greet(before)
+        greet(after)
+
+    @pl.when(crossing)
+    def _():
+        greet(0)
+        greet(members - 1)
 
     def rightward(r, c):
         return pltpu.make_async_remote_copy(
@@ -128,12 +147,52 @@
         return pltpu.make_async_copy(
             upper.at[r, rows(c)], lower.at[r + 1, rows(c)], come_sem.at[1, r, c])
 
+    def detour(r, c, toward):
+        by_last = lax.rem(c + toward, 2) == 0
+        return pltpu.make_async_remote_copy(
+            (lower if toward else upper).at[r, rows(c)], relay.at[r, rows(c)],
+            sent_sem.at[toward, r, c], relay_come.at[r, c],
+            device_id={"tour": jnp.where(by_last, members - 1, 0)}, device_id_type=MESH)
+
+    def forward(r, c, toward):
+        return pltpu.make_async_remote_copy(
+            relay.at[r, rows(c)], (lower if toward else upper).at[r + 1, rows(c)],
+            relay_sent.at[r, c], come_sem.at[toward, r, c],
+            device_id={"tour": before if toward else after}, device_id_type=MESH)
+
+    def forwarded_left(c):
+        return lax.rem(c + jnp.where(first, 1, 0), 2) == 1
+
+    def pass_on(r):
+        def step(c, _):
+            arrival(r, c).wait_recv()
+
+            @pl.when(forwarded_left(c))
+            def _():
+                forward(r, c, 1).start()
+
+            @pl.when(jnp.logical_not(forwarded_left(c)))
+            def _():
+                forward(r, c, 0).start()
+
+            return 0
+        return step
+
+    def arrival(r, c):
+        return pltpu.make_async_remote_copy(
+            relay.at[r, rows(c)], relay.at[r, rows(c)], relay_sent.at[r, c], relay_come.at[r, c],
+            device_id={"tour": before}, device_id_type=MESH)
+
     def send(r, c):
         @pl.when(last)
         def _():
             turn_last(r, c).start()
 
-        @pl.when(jnp.logical_not(last))
+        @pl.when(leaves_right)
+        def _():
+            detour(r, c, 0).start()
+
+        @pl.when(next_door)
         def _():
             rightward(r, c).start()
 
@@ -141,7 +200,11 @@
         def _():
             turn_first(r, c).start()
 
-        @pl.when(jnp.logical_not(first))
+        @pl.when(leaves_left)
+        def _():
+            detour(r, c, 1).start()
+
+        @pl.when(next_back)
         def _():
             leftward(r, c).start()
 
@@ -260,11 +323,11 @@
 
         @pl.when(r == 0)
         def _():
-            @pl.when(jnp.logical_or(first, last))
-            def _():
-                pl.semaphore_wait(barrier, 4)
-
-            @pl.when(jnp.logical_not(jnp.logical_or(first, last)))
+            @pl.when(jnp.logical_or(ends, crossing))
+            def _():
+                pl.semaphore_wait(barrier, 6)
+
+            @pl.when(jnp.logical_not(jnp.logical_or(ends, crossing)))
             def _():
                 pl.semaphore_wait(barrier, 5)
 
@@ -278,30 +341,18 @@
 
         for k in range(3):
             swap_gram(r, k).wait_recv()
-
-        @pl.when(jnp.logical_and(crossing, r > 0))
-        def _():
-            lax.fori_loop(chunks, every, vector_step(r - 1), 0)
-
         gram = (grams[r, 0] + grams[r, 1]) + (grams[r, 2] + grams[r, 3])
         spun[0], spun[1] = split(spread_out(rotation_of(gram)))
         lax.fori_loop(0, chunks, matrix_step(r), 0)
-
-        @pl.when(jnp.logical_not(crossing))
-        def _():
-            lax.fori_loop(chunks, every, vector_step(r), 0)
+        lax.fori_loop(chunks, every, vector_step(r), 0)
+
+        @pl.when(ends)
+        def _():
+            lax.fori_loop(0, every, pass_on(r), 0)
 
         return 0
 
     lax.fori_loop(0, ROUNDS, one_round, 0)
-
-    @pl.when(crossing)
-    def _():
-        lax.fori_loop(chunks, every, vector_step(ROUNDS - 1), 0)
-
-    def store(c, half):
-        piece = staged(c)[half]
-        return piece
 
     def finish(kind, out, offset):
         def step(c, _):
@@ -336,13 +387,25 @@
             swap_gram(r, k).wait_send()
 
         def step(c, _):
-            @pl.when(jnp.logical_not(last))
+            @pl.when(next_door)
             def _():
                 rightward(r, c).wait_send()
 
-            @pl.when(jnp.logical_not(first))
+            @pl.when(leaves_right)
+            def _():
+                detour(r, c, 0).wait_send()
+
+            @pl.when(next_back)
             def _():
                 leftward(r, c).wait_send()
+
+            @pl.when(leaves_left)
+            def _():
+                detour(r, c, 1).wait_send()
+
+            @pl.when(ends)
+            def _():
+                arrival(r, c).wait_send()
 
             return 0
 
@@ -370,6 +433,7 @@
             pltpu.VMEM((ROUNDS + 1, tall + flat, WIDE), jnp.float32),
             pltpu.VMEM((ROUNDS + 1, tall + flat, WIDE), jnp.float32),
             pltpu.VMEM((2 * (tall + flat), WIDE), jnp.float32),
+            pltpu.VMEM((ROUNDS, tall + flat, WIDE), jnp.float32),
             pltpu.VMEM((2 * WIDE, 4 * WIDE), jnp.float32),
             pltpu.VMEM((2, 2 * WIDE, 2 * WIDE), jnp.bfloat16),
             pltpu.VMEM((ROUNDS, 4, WIDE, WIDE), jnp.float32),
@@ -377,6 +441,8 @@
             pltpu.SemaphoreType.DMA((2, every)),
             pltpu.SemaphoreType.DMA((2, ROUNDS, every)),
             pltpu.SemaphoreType.DMA((2, ROUNDS, every)),
+            pltpu.SemaphoreType.DMA((ROUNDS, every)),
+            pltpu.SemaphoreType.DMA((ROUNDS, every)),
             pltpu.SemaphoreType.DMA((ROUNDS, 3)),
             pltpu.SemaphoreType.DMA((ROUNDS, 3)),
         ],

time: 283 us -> 228 us (0.81)
  Pallas kernels: 275 us -> 220 us
    pallas_call x1, Pallas kernels: 275 us -> 220 us  [local(): pl.pallas_call(kernel, out_shape=(jax.ShapeDtypeStruct(iterate.shape, jnp...]
where the time goes in v2:
time: 228 us; the launch traced here: 225 us
  Pallas kernels  220 us (96%)
  local copies, waits for them, and re-layouts  3.51 us (2%)
    pallas_call x1, Pallas kernels, local(): pl.pallas_call(kernel, out_shape=(jax.ShapeDtypeStruct(iterate.shape, jnp...  220 us

profile of v2, /device:TPU:4, one launch (start us, length us, event | category | flops | bytes accessed | tf_op | source)
XLA Modules:
  0.0 224.6 jit_solution(11122490300764690034)
XLA Ops:
  0.6 0.0 copy-start
  0.6 1.2 copy-done
  1.9 220.5 %shard_map.41 = (f32[4096,128]{1,0:T(8,128)S(1)}, f32[2048,128]{1,0:T(8,128)S(1)}) custom-call(f32[4096,128]{1,0:T(8,128)} %matrix_in.1, f32[2048,128]{1,0:T(8,128)S(1)} %copy-done), custom_call_target="tpu_custom_call" | custom-call | flops 9663676416 | bytes 12582912 | tf_op jit(solution)/shard_map/pallas_call | solution.py:424
  222.3 1.3 copy.6
  223.7 1.0 copy.7
Async XLA Ops:
  0.6 1.2 copy-start

commit v3 on v2

--- a/solution.py
+++ b/solution.py
@@ -261,6 +261,23 @@
                 pltpu.roll(right[one], HALF, 1) + right[two]))
         return jnp.concatenate(parts, axis=0)
 
+    near_quarter = near_square[: HALF // 2]
+
+    def packed(gram):
+        top, bottom = gram[:HALF], gram[HALF:]
+        corner = jnp.where(
+            near_quarter, pltpu.roll(top[: HALF // 2], HALF, 1), top[HALF // 2 :])
+        return jnp.concatenate([jnp.where(near_square, top, bottom), corner], axis=0)
+
+    def unpacked(pieces):
+        ends_of, corner = pieces[:HALF], pieces[HALF:]
+        beside = jnp.concatenate([pltpu.roll(corner, HALF, 1), corner], axis=0)
+        upper_part = jnp.concatenate(
+            [jnp.where(near_square, ends_of, beside), jnp.where(near_square, 0.0, ends_of)], axis=0)
+        mirrored = upper_part.T
+        return jnp.concatenate(
+            [upper_part[:HALF], jnp.where(near_square, mirrored[HALF:], upper_part[HALF:])], axis=0)
+
     def swap_gram(r, k):
         return pltpu.make_async_remote_copy(
             grams.at[r, share], grams.at[r, share], gram_sent.at[r, k], gram_come.at[r, k],
@@ -319,7 +336,7 @@
         sums[...] = jnp.zeros_like(sums)
         lax.fori_loop(0, chunks, gram_step(r), 0)
         cross = folded(2 * WIDE)
-        grams[r, share] = folded(0) + (cross + cross.T)
+        grams[r, share] = packed(folded(0) + (cross + cross.T))
 
         @pl.when(r == 0)
         def _():
@@ -341,7 +358,7 @@
 
         for k in range(3):
             swap_gram(r, k).wait_recv()
-        gram = (grams[r, 0] + grams[r, 1]) + (grams[r, 2] + grams[r, 3])
+        gram = unpacked((grams[r, 0] + grams[r, 1]) + (grams[r, 2] + grams[r, 3]))
         spun[0], spun[1] = split(spread_out(rotation_of(gram)))
         lax.fori_loop(0, chunks, matrix_step(r), 0)
         lax.fori_loop(chunks, every, vector_step(r), 0)
@@ -436,7 +453,7 @@
             pltpu.VMEM((ROUNDS, tall + flat, WIDE), jnp.float32),
             pltpu.VMEM((2 * WIDE, 4 * WIDE), jnp.float32),
             pltpu.VMEM((2, 2 * WIDE, 2 * WIDE), jnp.bfloat16),
-            pltpu.VMEM((ROUNDS, 4, WIDE, WIDE), jnp.float32),
+            pltpu.VMEM((ROUNDS, 4, HALF + HALF // 2, WIDE), jnp.float32),
             pltpu.SemaphoreType.DMA((2,)),
             pltpu.SemaphoreType.DMA((2, every)),
             pltpu.SemaphoreType.DMA((2, ROUNDS, every)),

time: 228 us -> 227 us (level)
  no operation moved by 1% of the time
where the time goes in v3:
time: 227 us; the launch traced here: 224 us
  Pallas kernels  220 us (97%)
  local copies, waits for them, and re-layouts  3.51 us (2%)
    pallas_call x1, Pallas kernels, local(): pl.pallas_call(kernel, out_shape=(jax.ShapeDtypeStruct(iterate.shape, jnp...  220 us

profile of v3, /device:TPU:4, one launch (start us, length us, event | category | flops | bytes accessed | tf_op | source)
XLA Modules:
  0.0 223.9 jit_solution(2005030189847432278)
XLA Ops:
  0.6 0.0 copy-start
  0.6 1.2 copy-done
  1.9 219.8 %shard_map.41 = (f32[4096,128]{1,0:T(8,128)S(1)}, f32[2048,128]{1,0:T(8,128)S(1)}) custom-call(f32[4096,128]{1,0:T(8,128)} %matrix_in.1, f32[2048,128]{1,0:T(8,128)S(1)} %copy-done), custom_call_target="tpu_custom_call" | custom-call | flops 9663676416 | bytes 12582912 | tf_op jit(solution)/shard_map/pallas_call | solution.py:441
  221.6 1.3 copy.6
  223.0 1.0 copy.7
Async XLA Ops:
  0.6 1.2 copy-start
